TPU v7x, 32 devices: a whole 2x2x4 slice. The times are simulated.
32 devices in a mesh: gx: 4 (over z), gy: 8 (over y, x, core).
Axes of the slice: x: 2, y: 2, z: 4, core: 2. Of those that a mesh axis runs over, the one named last changes fastest.
Arguments:
- tokens: bfloat16 [8192, 1664], P('gy', 'gx'), may hold values from -6 to 6
- segment_ids: int32 [8192], P('gy'), may hold values from 0 to 255, as said below
- first_gain: float32 [1664], replicated, may hold values from 0.5 to 2
- first_bias: float32 [1664], replicated, may hold values from -3 to 3
- query_key_value: bfloat16 [3, 1664, 1664], P(None, 'gy', 'gx'), may hold values from -0.15625 to 0.15625
- project_out: bfloat16 [1664, 1664], P('gx', 'gy'), may hold values from -0.15625 to 0.15625
- second_gain: float32 [1664], replicated, may hold values from 0.5 to 2
- second_bias: float32 [1664], replicated, may hold values from -3 to 3
- up_weight: bfloat16 [1664, 8192], P('gy', 'gx'), may hold values from -0.15625 to 0.15625
- down_weight: bfloat16 [8192, 1664], P('gx', 'gy'), may hold values from -0.0625 to 0.0625
- final_gain: float32 [1664], replicated, may hold values from 0.5 to 2
- final_bias: float32 [1664], replicated, may hold values from -3 to 3
- merge_weight: bfloat16 [4, 1664, 1664], P(None, 'gx', 'gy'), may hold values from -0.078125 to 0.078125
- owners: int32 [2048, 1], P('gy'), may hold values from 0 to 7; in each aligned block of 256 rows (0 to 255, 256 to 511, ...) at most 64 rows name the same one
Outputs:
- delivered: bfloat16 [8, 8, 64, 1664], P('gy', None, None, 'gx')
Inputs may be any that keep to these rules, and one draw needn't show every extreme that they name: `segment_ids`: each segment is a run of whole units of 32 consecutive tokens that lies inside one aligned block of 1024 tokens; ids never fall along the tokens and differ between segments. `owners`: in each aligned block of 256 rows (the merged tokens of one index of gy), no owner is named by more than 64 rows.
All inputs are finite; a program needn't handle non-finite values.
Results may differ from a plain program's by a relative error of at most 0.02.
Values may be sent and summed in bfloat16 or wider, within the bound.
A program may use at most 128 MiB of HBM per device.

v0:
```python
import jax
import jax.numpy as jnp
from jax import lax
from jax.sharding import PartitionSpec as P

HEAD = 104
IMG_W = 16


EPSILON = 1e-06


def normalize_rows(values, gain, bias):
    values = values.astype(jnp.float32)
    center = values - jnp.mean(values, axis=-1, keepdims=True)
    spread = jnp.mean(center * center, axis=-1, keepdims=True)
    return center * lax.rsqrt(spread + EPSILON) * gain + bias


def normalize_from_sums(values, sums, features, gain, bias):
    values = values.astype(jnp.float32)
    row_mean = sums[0] / features
    spread = sums[1] / features - row_mean * row_mean
    return (values - row_mean[:, None]) * lax.rsqrt(spread[:, None] + EPSILON) * gain + bias


def own_slice(vector, width):
    return lax.dynamic_slice_in_dim(vector, lax.axis_index("gx") * width, width, 0)


def row_sums(values):
    values = values.astype(jnp.float32)
    return (jnp.sum(values, axis=-1), jnp.sum(values * values, axis=-1))


def local_attention(qkv, segment_ids):
    tok_rows = qkv.shape[1]
    head_count = qkv.shape[2] // HEAD
    queries = qkv[0].reshape(tok_rows, head_count, HEAD)
    key_rows = qkv[1].reshape(tok_rows, head_count, HEAD)
    value_rows = qkv[2].reshape(tok_rows, head_count, HEAD)
    query_block = min(512, tok_rows)

    def one_block(index):
        first_query = index * query_block
        query_part = lax.dynamic_slice_in_dim(queries, first_query, query_block, 0)
        query_ids = lax.dynamic_slice_in_dim(segment_ids, first_query, query_block, 0)
        scores = jnp.einsum(
            "qhe,khe->hqk", query_part, key_rows, preferred_element_type=jnp.float32
        ) * HEAD ** (-0.5)
        same_segment = query_ids[None, :, None] == segment_ids[None, None, :]
        scores = jnp.where(same_segment, scores, -1e30)
        highest = jnp.max(scores, axis=-1, keepdims=True)
        raised = jnp.exp(scores - highest)
        shares = (raised / jnp.sum(raised, axis=-1, keepdims=True)).astype(jnp.bfloat16)
        return jnp.einsum(
            "hqk,khe->qhe", shares, value_rows, preferred_element_type=jnp.float32
        ).astype(jnp.bfloat16)

    blocks = lax.map(one_block, jnp.arange(tok_rows // query_block, dtype=jnp.int32))
    return blocks.reshape(tok_rows, head_count * HEAD)


def body(
    tokens,
    segment_ids,
    first_gain,
    first_bias,
    query_key_value,
    project_out,
    second_gain,
    second_bias,
    up_weight,
    down_weight,
    final_gain,
    final_bias,
    merge_weight,
    owners,
):
    tok_rows = tokens.shape[0]
    feature_cols = tokens.shape[1]
    features = feature_cols * lax.axis_size("gx")
    full_rows = lax.all_gather(tokens, "gx", axis=1, tiled=True)
    normed = normalize_rows(full_rows, first_gain, first_bias).astype(jnp.bfloat16)
    columns = normed
    qkv = jnp.einsum(
        "td,kdc->ktc",
        columns,
        lax.all_gather(query_key_value, "gy", axis=1, tiled=True),
        preferred_element_type=jnp.float32,
    ).astype(jnp.bfloat16)
    attended = local_attention(qkv, segment_ids)
    out_terms = jnp.dot(
        attended,
        lax.all_gather(project_out, "gy", axis=1, tiled=True),
        preferred_element_type=jnp.float32,
    )
    attn_share = lax.psum_scatter(
        out_terms.astype(jnp.bfloat16), "gx", scatter_dimension=1, tiled=True
    ).astype(jnp.float32)
    first_resid = (tokens.astype(jnp.float32) + attn_share).astype(jnp.bfloat16)
    resid_rows = lax.all_gather(first_resid, "gx", axis=1, tiled=True)
    second_normed = normalize_rows(resid_rows, second_gain, second_bias).astype(jnp.bfloat16)
    columns = second_normed
    upper = jnp.dot(
        columns,
        lax.all_gather(up_weight, "gy", axis=0, tiled=True),
        preferred_element_type=jnp.float32,
    )
    hidden = jax.nn.gelu(upper, approximate=False).astype(jnp.bfloat16)
    down_terms = jnp.dot(
        hidden,
        lax.all_gather(down_weight, "gy", axis=1, tiled=True),
        preferred_element_type=jnp.float32,
    )
    mlp_share = lax.psum_scatter(
        down_terms.astype(jnp.bfloat16), "gx", scatter_dimension=1, tiled=True
    ).astype(jnp.float32)
    second_resid = (first_resid.astype(jnp.float32) + mlp_share).astype(jnp.bfloat16)
    post_sums = lax.psum(row_sums(second_resid), "gx")
    final_normed = normalize_from_sums(
        second_resid,
        post_sums,
        features,
        own_slice(final_gain, feature_cols),
        own_slice(final_bias, feature_cols),
    ).astype(jnp.bfloat16)
    merged_rows = tok_rows // 4
    grouped = (
        final_normed.reshape(tok_rows // (2 * IMG_W), 2, IMG_W // 2, 2, feature_cols)
        .transpose(0, 2, 1, 3, 4)
        .reshape(merged_rows, 4, feature_cols)
    )
    merge_terms = jnp.einsum(
        "pkf,kfc->pc",
        grouped,
        lax.all_gather(merge_weight, "gy", axis=2, tiled=True),
        preferred_element_type=jnp.float32,
    )
    projected = lax.psum_scatter(
        merge_terms.astype(jnp.bfloat16), "gx", scatter_dimension=1, tiled=True
    )
    owner_count = lax.axis_size("gy")
    capacity = max(2, 2 * merged_rows // owner_count)
    owner_col = owners[:, 0]
    one_hot = (owner_col[:, None] == jnp.arange(owner_count, dtype=jnp.int32)[None, :]).astype(
        jnp.int32
    )
    slot_rank = jnp.sum((jnp.cumsum(one_hot, axis=0) - 1) * one_hot, axis=1)
    outgoing = (
        jnp.zeros((owner_count, capacity, feature_cols), jnp.bfloat16)
        .at[owner_col, slot_rank]
        .set(projected)
    )
    arrived = lax.all_to_all(outgoing, "gy", split_axis=0, concat_axis=0, tiled=True)
    return arrived.reshape(1, owner_count, capacity, feature_cols)


def solution(mesh):
    in_specs = (
        P("gy", "gx"),
        P("gy"),
        P(),
        P(),
        P(None, "gy", "gx"),
        P("gx", "gy"),
        P(),
        P(),
        P("gy", "gx"),
        P("gx", "gy"),
        P(),
        P(),
        P(None, "gx", "gy"),
        P("gy", None),
    )
    out_specs = P("gy", None, None, "gx")
    return jax.shard_map(body, mesh=mesh, in_specs=in_specs, out_specs=out_specs, check_vma=False)
```

profile of v0, /device:TPU:0, one launch (start us, length us, event | category | flops | bytes accessed | tf_op | source)
XLA Modules:
  0.0 595.7 jit_solution(17590873093442585721)
XLA Ops:
  11.8 67.7 %all-gather.8.cloned.1.call-done = bf16[1024,1664]{0,1:T(8,128)(2,1)} async-done(((bf16[1024,416]{0,1:T(8,128)(2,1)}), bf16[1024,1664]{0,1:T(8,128)(2,1)}) %all-gather.8.cloned.1.call-update) | async-done | bytes 3407888 | tf_op jit(solution)/shard_map/all_gather | solution.py:83
  82.2 2.9 fusion.42
  85.2 42.6 %all-gather.10.cloned.1.call-done = bf16[3,1664,416]{2,0,1:T(4,128)(2,1)} async-done(((bf16[3,208,416]{2,0,1:T(4,128)(2,1)}), bf16[3,1664,416]{2,0,1:T(4,128)(2,1)}) %all-gather.10.cloned.1.call-update) | async-done | bytes 4153360 | tf_op jit(solution)/shard_map/all_gather | solution.py:89
  127.8 8.7 %convert_bitcast_fusion = bf16[3,1024,416]{1,2,0:T(8,128)(2,1)S(1)} fusion(bf16[3,1664,416]{2,0,1:T(4,128)(2,1)} %all-gather.10.cloned.1.call-done, bf16[1024,1664]{0,1:T(8,128)(2,1)S(1)} %copy-done.1, f32[1664]{0:T(1024)S(1)} %copy-done.7, f32[1664]{0:T(1024)S(1)} %copy-done.8, f32[1024]{0:T(1024)S(1)} %add_rsqrt_fusion.2, ...), kind=kOutput, calls=%fused_computation.77 | convolution fusion | flops 4264525824 | bytes 10138624 | tf_op jit(solution)/shard_map/td,kdc->ktc/dot_general | solution.py:86
  136.7 26.2 %while.10 = (s32[]{:T(128)}, bf16[2,512,4,104]{1,3,2,0:T(8,128)(2,1)}, s32[2]{0:T(128)S(1)}, s32[1024]{0:T(1024)S(1)}, bf16[1024,4,104]{0,2,1:T(8,128)(2,1)S(1)}...) while((s32[]{:T(128)}, ...), condition=%wide.region_8.9_spmd, body=%wide.region_5.8_spmd.sunk | while | flops 885736448 | bytes 20409008 | solution.py:60
  138.9 5.5 fusion.150
  144.4 5.7 fusion.151
  151.7 5.5 fusion.150
  157.3 5.7 fusion.151
  165.2 5.2 convolution_convert_fusion
  170.5 64.4 %reduce-scatter.4.cloned.1.call-done = bf16[1024,416]{0,1:T(8,128)(2,1)} async-done(((bf16[1024,1664]{0,1:T(8,128)(2,1)}), bf16[1024,416]{0,1:T(8,128)(2,1)}) %reduce-scatter.4.cloned.1.call-update) | async-done | bytes 851984 | tf_op jit(solution)/shard_map/reduce_scatter | solution.py:98
  238.9 66.6 %all-gather.14.cloned.1.call-done = bf16[1024,1664]{0,1:T(8,128)(2,1)} async-done(((bf16[1024,416]{0,1:T(8,128)(2,1)}), bf16[1024,1664]{0,1:T(8,128)(2,1)}) %all-gather.14.cloned.1.call-update) | async-done | bytes 3407888 | tf_op jit(solution)/shard_map/all_gather | solution.py:102
  308.2 2.9 fusion.38
  311.2 42.5 %all-gather.16.cloned.1.call-done = bf16[1664,2048]{1,0:T(8,128)(2,1)} async-done(((bf16[208,2048]{1,0:T(8,128)(2,1)}), bf16[1664,2048]{1,0:T(8,128)(2,1)}) %all-gather.16.cloned.1.call-update) | async-done | bytes 6815760 | tf_op jit(solution)/shard_map/all_gather | solution.py:107
  353.6 31.2 %fusion.140 = bf16[1024,2048]{1,0:T(8,128)(2,1)} fusion(bf16[1664,2048]{1,0:T(8,128)(2,1)} %all-gather.16.cloned.1.call-done, bf16[1024,1664]{0,1:T(8,128)(2,1)S(1)} %copy-done.2, f32[1664]{0:T(1024)S(1)} %copy-done.9, f32[1664]{0:T(1024)S(1)} %copy-done.10, f32[1024]{0:T(1024)S(1)} %add_rsqrt_fusion.1, ...), kind=kOutput, calls=%fused_computation.29.clone.clone.clone.clone.1 | convolution fusion | flops 7125860352 | bytes 14439424 | tf_op jit(solution)/shard_map/dot_general | solution.py:105
  384.8 18.5 %all-gather.18.cloned.1.call-done = bf16[2048,1664]{0,1:T(8,128)(2,1)} async-done(((bf16[2048,208]{0,1:T(8,128)(2,1)}), bf16[2048,1664]{0,1:T(8,128)(2,1)}) %all-gather.18.cloned.1.call-update) | async-done | bytes 6815760 | tf_op jit(solution)/shard_map/all_gather | solution.py:113
  403.3 11.9 %fusion.50 = bf16[1024,1664]{0,1:T(8,128)(2,1)} fusion(bf16[2048,1664]{0,1:T(8,128)(2,1)} %all-gather.18.cloned.1.call-done, bf16[1024,2048]{1,0:T(8,128)(2,1)} %fusion.140), kind=kOutput, calls=%fused_computation.60 | convolution fusion | flops 6981025792 | bytes 14417920 | tf_op jit(solution)/shard_map/dot_general | solution.py:111
  418.2 61.5 %reduce-scatter.6.cloned.1.call-done = bf16[1024,416]{0,1:T(8,128)(2,1)} async-done(((bf16[1024,1664]{0,1:T(8,128)(2,1)}), bf16[1024,416]{0,1:T(8,128)(2,1)}) %reduce-scatter.6.cloned.1.call-update) | async-done | bytes 851984 | tf_op jit(solution)/shard_map/reduce_scatter | solution.py:116
  481.3 10.8 %all-reduce = (f32[1024]{0:T(1024)S(1)}, f32[1024]{0:T(1024)S(1)}) all-reduce(f32[1024]{0:T(1024)S(1)} %get-tuple-element.44, f32[1024]{0:T(1024)S(1)} %get-tuple-element.43), channel_id=1, replica_groups=mesh['gx'=4,'gy'=8] {'gx'}, use_global_device_ids=true, to_apply=%region_16.17 | all-reduce | flops 2048 | bytes 16384 | tf_op jit(solution)/shard_map/psum | solution.py:120
  494.9 34.7 %all-gather.20.cloned.1.call-done = bf16[4,416,1664]{1,2,0:T(8,128)(2,1)} async-done(((bf16[4,416,208]{1,2,0:T(8,128)(2,1)}), bf16[4,416,1664]{1,2,0:T(8,128)(2,1)}) %all-gather.20.cloned.1.call-update) | async-done | bytes 5537808 | tf_op jit(solution)/shard_map/all_gather | solution.py:137
  529.6 5.8 fusion.73
  536.4 23.3 %reduce-scatter.8.cloned.1.call-done = bf16[256,416]{0,1:T(8,128)(2,1)} async-done(((bf16[256,1664]{0,1:T(8,128)(2,1)}), bf16[256,416]{0,1:T(8,128)(2,1)}) %reduce-scatter.8.cloned.1.call-update) | async-done | bytes 213008 | tf_op jit(solution)/shard_map/reduce_scatter | solution.py:140
  560.9 13.8 %scatter_fusion = bf16[8,64,416]{2,1,0:T(8,128)(2,1)S(1)} fusion(bf16[8,64,416]{2,1,0:T(8,128)(2,1)S(1)} %broadcast_in_dim.24, s32[256]{0:T(256)S(1)} %bitcast.61, bf16[256,416]{1,0:T(8,128)(2,1)S(1)} %copy.36), kind=kCustom, calls=%fused_computation | custom fusion | bytes 641024 | tf_op jit(solution)/shard_map/scatter | solution.py:153
  574.7 13.2 %all_to_all.5 = bf16[8,64,416]{2,1,0:T(8,128)(2,1)S(1)} all-to-all(bf16[8,64,416]{2,1,0:T(8,128)(2,1)S(1)} %scatter_fusion), channel_id=1, replica_groups=mesh['gx'=4,'gy'=8] {'gy'}, dimensions={0} | all-to-all | bytes 851968 | tf_op jit(solution)/shard_map/all_to_all | solution.py:155
  (82 shorter events, 29.4 us)
Async XLA Ops:
  6.5 121.2 %copy-start.8 = (f32[1664]{0:T(1024)S(1)}, f32[1664]{0:T(1024)}, u32[]{:S(2)}) copy-start(f32[1664]{0:T(1024)} %param.18) | copy-start | bytes 19972
  6.5 121.2 %copy-start.7 = (f32[1664]{0:T(1024)S(1)}, f32[1664]{0:T(1024)}, u32[]{:S(2)}) copy-start(f32[1664]{0:T(1024)} %param.19) | copy-start | bytes 19972
  6.5 73.0 %all-gather.8.cloned.1.call-start = ((), (), s32[]{:S(2)}) async-start(), calls=%async_computation.4 | async-start | bytes 4259840 | tf_op jit(solution)/shard_map/all_gather | solution.py:83
  7.3 120.5 %all-gather.10.cloned.1.call-start = ((), (), s32[]{:S(2)}) async-start(), calls=%async_computation.5 | async-start | bytes 7667712 | tf_op jit(solution)/shard_map/all_gather | solution.py:89
  9.9 155.2 %all-gather.12.cloned.1.call-start = ((), (), s32[]{:S(2)}) async-start(), calls=%async_computation.6 | async-start | bytes 1916928 | tf_op jit(solution)/shard_map/all_gather | solution.py:95
  11.8 223.1 %reduce-scatter.4.cloned.1.call-start = ((), (), s32[]{:S(2)}) async-start(), calls=%async_computation.7 | async-start | bytes 4259840 | tf_op jit(solution)/shard_map/reduce_scatter | solution.py:98
  79.5 48.3 %copy-start.1 = (bf16[1024,1664]{0,1:T(8,128)(2,1)S(1)}, bf16[1024,1664]{0,1:T(8,128)(2,1)}, u32[]{:S(2)}) copy-start(bf16[1024,1664]{0,1:T(8,128)(2,1)} %all-gather.8.cloned.1.call-done) | copy-start | bytes 10223620
  85.2 51.6 %copy-start.5 = (s32[1024]{0:T(1024)S(1)}, s32[1024]{0:T(1024)}, u32[]{:S(2)}) copy-start(s32[1024]{0:T(1024)} %param.17) | copy-start | bytes 12292
  165.2 69.7 %copy-start.3 = (bf16[1024,416]{0,1:T(8,128)(2,1)S(1)}, bf16[1024,416]{0,1:T(8,128)(2,1)}, u32[]{:S(2)}) copy-start(bf16[1024,416]{0,1:T(8,128)(2,1)} %param.16) | copy-start | bytes 2555908
  170.4 183.2 %copy-start.9 = (f32[1664]{0:T(1024)S(1)}, f32[1664]{0:T(1024)}, u32[]{:S(2)}) copy-start(f32[1664]{0:T(1024)} %param.23) | copy-start | bytes 19972
  170.4 183.2 %copy-start.10 = (f32[1664]{0:T(1024)S(1)}, f32[1664]{0:T(1024)}, u32[]{:S(2)}) copy-start(f32[1664]{0:T(1024)} %param.22) | copy-start | bytes 19972
  170.4 135.1 %all-gather.14.cloned.1.call-start = ((), (), s32[]{:S(2)}) async-start(), calls=%async_computation.8 | async-start | bytes 4259840 | tf_op jit(solution)/shard_map/all_gather | solution.py:102
  237.3 116.3 %all-gather.16.cloned.1.call-start = ((), (), s32[]{:S(2)}) async-start(), calls=%async_computation.9 | async-start | bytes 7667712 | tf_op jit(solution)/shard_map/all_gather | solution.py:107
  237.9 165.4 %all-gather.18.cloned.1.call-start = ((), (), s32[]{:S(2)}) async-start(), calls=%async_computation.10 | async-start | bytes 7667712 | tf_op jit(solution)/shard_map/all_gather | solution.py:113
  238.6 241.1 %reduce-scatter.6.cloned.1.call-start = ((), (), s32[]{:S(2)}) async-start(), calls=%async_computation.11 | async-start | bytes 4259840 | tf_op jit(solution)/shard_map/reduce_scatter | solution.py:116
  305.5 48.1 %copy-start.2 = (bf16[1024,1664]{0,1:T(8,128)(2,1)S(1)}, bf16[1024,1664]{0,1:T(8,128)(2,1)}, u32[]{:S(2)}) copy-start(bf16[1024,1664]{0,1:T(8,128)(2,1)} %all-gather.14.cloned.1.call-done) | copy-start | bytes 10223620
  384.8 30.5 %copy-start.4 = (bf16[4,416,208]{2,1,0:T(8,128)(2,1)S(1)}, bf16[4,416,208]{2,1,0:T(8,128)(2,1)}, u32[]{:S(2)}) copy-start(bf16[4,416,208]{2,1,0:T(8,128)(2,1)} %param.28) | copy-start | bytes 2076676
  384.8 94.9 %copy-start = (bf16[1024,416]{0,1:T(8,128)(2,1)S(1)}, bf16[1024,416]{0,1:T(8,128)(2,1)}, u32[]{:S(2)}) copy-start(bf16[1024,416]{0,1:T(8,128)(2,1)} %add_convert_fusion.1) | copy-start | bytes 2555908
  415.2 114.4 %all-gather.20.cloned.1.call-start = ((), (), s32[]{:S(2)}) async-start(), calls=%async_computation.12 | async-start | bytes 7667712 | tf_op jit(solution)/shard_map/all_gather | solution.py:137
  416.6 143.2 %reduce-scatter.8.cloned.1.call-start = ((), (), s32[]{:S(2)}) async-start(), calls=%async_computation.13 | async-start | bytes 1064960 | tf_op jit(solution)/shard_map/reduce_scatter | solution.py:140
  494.7 40.8 %copy-start.6 = (s32[256,1]{0,1:T(1,128)S(1)}, s32[256,1]{0,1:T(1,128)}, u32[]{:S(2)}) copy-start(s32[256,1]{0,1:T(1,128)} %param.29) | copy-start | bytes 3076
Sparse Core Ops, SparseCore 0:
  8.9 70.5 all-gather.7
  81.4 46.3 all-gather.9
  129.7 26.2 all-gather.11
  170.5 64.3 reduce-scatter.3
  237.4 68.0 all-gather.13
  307.2 46.3 all-gather.15
  355.5 47.7 all-gather.17
  415.4 64.3 reduce-scatter.5
  481.6 47.9 all-gather.19
  535.6 24.1 reduce-scatter.7
where the time goes:
time: 603 us; the launch traced here: 596 us
  waiting for transfers between devices  424 us (70%)
  matrix products  85.2 us (14%)
  local copies, waits for them, and re-layouts  28 us (5%)
  blocking collectives  24 us (4%)
  other arithmetic  18.3 us (3%)
  between operations  13.9 us (2%)
    all_gather x1, waiting for transfers between devices, body(): full_rows = lax.all_gather(tokens, 'gx', axis=1, tiled=True)  67.7 us
    all_gather x1, waiting for transfers between devices, body(): resid_rows = lax.all_gather(first_resid, 'gx', axis=1, tiled=True)  66.6 us
    reduce_scatter x1, waiting for transfers between devices, body(): lax.psum_scatter(out_terms.astype(jnp.bfloat16), 'gx', scatter_dimension=...  64.4 us
    reduce_scatter x1, waiting for transfers between devices, body(): lax.psum_scatter(down_terms.astype(jnp.bfloat16), 'gx', scatter_dimension...  61.5 us
    all_gather x1, waiting for transfers between devices, body(): lax.all_gather(query_key_value, 'gy', axis=1, tiled=True)  42.6 us
    all_gather x1, waiting for transfers between devices, body(): lax.all_gather(up_weight, 'gy', axis=0, tiled=True)  42.5 us
    all_gather x1, waiting for transfers between devices, body(): lax.all_gather(merge_weight, 'gy', axis=2, tiled=True)  34.7 us
    dot_general x1, matrix products, body(): jnp.dot(columns, lax.all_gather(up_weight, 'gy', axis=0, tiled=True), pre...  31.2 us
  transfers between devices with their start and end apart: 10, of which 9 were waited for; matrix products, arithmetic and copies ran while one was open for 15% of the time, Pallas kernels for 0%

commit v1 on v0

v1 whole, which is shorter than its diff:
```python
import jax
import jax.numpy as jnp
from jax import lax
from jax.sharding import PartitionSpec as P

HEAD = 104
IMG_W = 16
FIRST_CHUNKS = 2
MAIN_CHUNKS = 4


EPSILON = 1e-06


def normalize_rows(values, gain, bias):
    values = values.astype(jnp.float32)
    center = values - jnp.mean(values, axis=-1, keepdims=True)
    spread = jnp.mean(center * center, axis=-1, keepdims=True)
    return center * lax.rsqrt(spread + EPSILON) * gain + bias


def normalize_from_sums(values, sums, features, gain, bias):
    values = values.astype(jnp.float32)
    row_mean = sums[0] / features
    spread = sums[1] / features - row_mean * row_mean
    return (values - row_mean[:, None]) * lax.rsqrt(spread[:, None] + EPSILON) * gain + bias


def own_slice(vector, width):
    return lax.dynamic_slice_in_dim(vector, lax.axis_index("gx") * width, width, 0)


def row_sums(values):
    values = values.astype(jnp.float32)
    return jnp.stack([jnp.sum(values, axis=-1), jnp.sum(values * values, axis=-1)])


def line_gather(own):
    count = lax.axis_size("gx")
    place = lax.axis_index("gx")
    from_left, from_right = [own], [own]
    for step in range(1, count):
        up_pairs = [(i, i + 1) for i in range(step - 1, count - 1)]
        down_pairs = [(i, i - 1) for i in range(1, count - step + 1)]
        from_left.append(lax.ppermute(from_left[-1], "gx", up_pairs))
        from_right.append(lax.ppermute(from_right[-1], "gx", down_pairs))
    blocks = []
    for j in range(count):
        block = from_left[0]
        for i in range(count):
            if i != j:
                other = from_left[i - j] if i > j else from_right[j - i]
                block = jnp.where(place == i, other, block)
        blocks.append(block)
    return blocks


def line_scatter(term):
    count = lax.axis_size("gx")
    terms = {}

    def part(s):
        if s not in terms:
            terms[s] = term(s)
        return terms[s]

    rightward = leftward = None
    for step in range(1, count):
        up_sum = part(count - step)
        down_sum = part(step)
        if rightward is not None:
            up_sum = up_sum + rightward.astype(jnp.float32)
            down_sum = down_sum + leftward.astype(jnp.float32)
        rightward = lax.ppermute(
            up_sum.astype(jnp.bfloat16), "gx", [(i, i + 1) for i in range(step)]
        )
        leftward = lax.ppermute(
            down_sum.astype(jnp.bfloat16),
            "gx",
            [(i, i - 1) for i in range(count - step, count)],
        )
    total = part(0)
    if rightward is not None:
        total = total + rightward.astype(jnp.float32) + leftward.astype(jnp.float32)
    return total


def rows_for(weight_rows, s, width):
    count = lax.axis_size("gx")
    dest = lax.rem(lax.axis_index("gx") + s, count)
    return lax.dynamic_slice_in_dim(weight_rows, dest * width, width, 0)


def dot_rows(left, right):
    return lax.dot_general(
        left, right, (((1,), (1,)), ((), ())), preferred_element_type=jnp.float32
    )


def attend(queries, query_ids, key_rows, value_rows, segment_ids):
    scores = jnp.einsum(
        "qhe,khe->hqk", queries, key_rows, preferred_element_type=jnp.float32
    ) * HEAD ** (-0.5)
    same_segment = query_ids[None, :, None] == segment_ids[None, None, :]
    scores = jnp.where(same_segment, scores, -1e30)
    highest = jnp.max(scores, axis=-1, keepdims=True)
    raised = jnp.exp(scores - highest)
    total = jnp.sum(raised, axis=-1)
    mixed = jnp.einsum(
        "hqk,khe->qhe",
        raised.astype(jnp.bfloat16),
        value_rows,
        preferred_element_type=jnp.float32,
    )
    mixed = (mixed / total.T[:, :, None]).astype(jnp.bfloat16)
    return mixed.reshape(mixed.shape[0], -1)


def row_chunks(rows, wanted):
    unit = 2 * IMG_W
    count = wanted
    while count > 1 and rows % (count * unit):
        count //= 2
    return count, rows // count


def body(
    tokens,
    segment_ids,
    first_gain,
    first_bias,
    query_key_value,
    project_out,
    second_gain,
    second_bias,
    up_weight,
    down_weight,
    final_gain,
    final_bias,
    merge_weight,
    owners,
):
    tok_rows = tokens.shape[0]
    width = tokens.shape[1]
    features = width * lax.axis_size("gx")
    qkv_full = lax.all_gather(query_key_value, "gy", axis=1, tiled=True)
    out_rows = lax.all_gather(project_out.T, "gy", axis=0, tiled=True)
    up_full = lax.all_gather(up_weight, "gy", axis=0, tiled=True)
    down_rows = lax.all_gather(down_weight.T, "gy", axis=0, tiled=True)
    merge_rows = lax.all_gather(
        merge_weight.transpose(2, 0, 1).reshape(merge_weight.shape[2], 4 * width),
        "gy",
        axis=0,
        tiled=True,
    )

    count, size = row_chunks(tok_rows, FIRST_CHUNKS)
    qkv_parts = []
    for c in range(count):
        own = tokens[c * size : (c + 1) * size]
        full_rows = jnp.concatenate(line_gather(own), axis=1)
        normed = normalize_rows(full_rows, first_gain, first_bias).astype(jnp.bfloat16)
        qkv_parts.append(
            jnp.einsum(
                "td,kdc->ktc", normed, qkv_full, preferred_element_type=jnp.float32
            ).astype(jnp.bfloat16)
        )
    qkv = jnp.concatenate(qkv_parts, axis=1)
    head_count = qkv.shape[2] // HEAD
    queries = qkv[0].reshape(tok_rows, head_count, HEAD)
    key_rows = qkv[1].reshape(tok_rows, head_count, HEAD)
    value_rows = qkv[2].reshape(tok_rows, head_count, HEAD)

    count, size = row_chunks(tok_rows, MAIN_CHUNKS)
    projected_parts = []
    own_final_gain = own_slice(final_gain, width)
    own_final_bias = own_slice(final_bias, width)
    for c in range(count):
        rows = slice(c * size, (c + 1) * size)
        attended = attend(queries[rows], segment_ids[rows], key_rows, value_rows, segment_ids)
        attn_share = line_scatter(lambda s: dot_rows(attended, rows_for(out_rows, s, width)))
        first_resid = (tokens[rows].astype(jnp.float32) + attn_share).astype(jnp.bfloat16)
        resid_rows = jnp.concatenate(line_gather(first_resid), axis=1)
        second_normed = normalize_rows(resid_rows, second_gain, second_bias).astype(
            jnp.bfloat16
        )
        upper = jnp.dot(second_normed, up_full, preferred_element_type=jnp.float32)
        hidden = jax.nn.gelu(upper, approximate=False).astype(jnp.bfloat16)
        mlp_share = line_scatter(lambda s: dot_rows(hidden, rows_for(down_rows, s, width)))
        second_resid = (first_resid.astype(jnp.float32) + mlp_share).astype(jnp.bfloat16)
        post_sums = sum(line_gather(row_sums(second_resid)))
        final_normed = normalize_from_sums(
            second_resid, post_sums, features, own_final_gain, own_final_bias
        ).astype(jnp.bfloat16)
        grouped = (
            final_normed.reshape(size // (2 * IMG_W), 2, IMG_W // 2, 2, width)
            .transpose(0, 2, 1, 3, 4)
            .reshape(size // 4, 4 * width)
        )
        projected_parts.append(
            line_scatter(lambda s: dot_rows(grouped, rows_for(merge_rows, s, width))).astype(
                jnp.bfloat16
            )
        )
    projected = jnp.concatenate(projected_parts, axis=0)

    merged_rows = tok_rows // 4
    owner_count = lax.axis_size("gy")
    capacity = max(2, 2 * merged_rows // owner_count)
    owner_col = owners[:, 0]
    order = jnp.arange(merged_rows, dtype=jnp.int32)
    earlier = (owner_col[:, None] == owner_col[None, :]) & (order[None, :] < order[:, None])
    slot_rank = jnp.sum(earlier.astype(jnp.int32), axis=1)
    target = owner_col * capacity + slot_rank
    place = (
        jnp.arange(owner_count * capacity, dtype=jnp.int32)[:, None] == target[None, :]
    ).astype(jnp.bfloat16)
    outgoing = jnp.dot(place, projected, preferred_element_type=jnp.float32).astype(jnp.bfloat16)
    outgoing = outgoing.reshape(owner_count, capacity, width)
    arrived = lax.all_to_all(outgoing, "gy", split_axis=0, concat_axis=0, tiled=True)
    return arrived.reshape(1, owner_count, capacity, width)


def solution(mesh):
    in_specs = (
        P("gy", "gx"),
        P("gy"),
        P(),
        P(),
        P(None, "gy", "gx"),
        P("gx", "gy"),
        P(),
        P(),
        P("gy", "gx"),
        P("gx", "gy"),
        P(),
        P(),
        P(None, "gx", "gy"),
        P("gy", None),
    )
    out_specs = P("gy", None, None, "gx")
    return jax.shard_map(body, mesh=mesh, in_specs=in_specs, out_specs=out_specs, check_vma=False)
```

time: 603 us -> 606 us (level)
  starting transfers between devices: 0.55 us -> 209 us
  waiting for transfers between devices: 424 us -> 228 us
  blocking collectives: 24 us -> 13 us
    all_gather x7 -> x5, waiting for transfers between devices: 273 us -> 0.1 us  [the longest x1 0.02 us: body(): qkv_full = lax.all_gather(query_key_value, 'gy', axis=1, tiled=True)]
    ppermute x0 -> x132, waiting for transfers between devices: none -> 227 us  [the longest x36 120 us: line_scatter(): lax.ppermute(down_sum.astype(jnp.bfloat16), 'gx', [(i, i - 1) for i in ra...]
    ppermute x0 -> x132, starting transfers between devices: none -> 209 us  [the longest x36 80 us: line_scatter(): lax.ppermute(up_sum.astype(jnp.bfloat16), 'gx', [(i, i + 1) for i in rang...]
    reduce_scatter x3 -> x0, waiting for transfers between devices: 149 us -> none  [the longest x1 64.4 us: body(): lax.psum_scatter(out_terms.astype(jnp.bfloat16), 'gx', scatter_dimension=...]
    dot_general x7 -> x63, matrix products: 74.1 us -> 88.6 us  [the longest x48 36.7 us: dot_rows(): lax.dot_general(left, right, (((1,), (1,)), ((), ())), preferred_element_...]
    scatter x1 -> x0, local copies, waits for them, and re-layouts: 13.8 us -> none  [body(): outgoing = jnp.zeros((owner_count, capacity, feature_cols), jnp.bfloat16)...]
    all_gather x0 -> x1, local copies, waits for them, and re-layouts: none -> 11.3 us  [body(): qkv_full = lax.all_gather(query_key_value, 'gy', axis=1, tiled=True)]
    sub x2 -> x0, matrix products: 11 us -> none  [one_block(): raised = jnp.exp(scores - highest)]
  transfers between devices with their start and end apart: 10 -> 137, of which waited for: 9 -> 36; matrix products, arithmetic and copies ran while one was open for 15% -> 21% of each run, Pallas kernels for 0% -> 0%
where the time goes in v1:
time: 606 us; the launch traced here: 599 us
  waiting for transfers between devices  228 us (38%)
  starting transfers between devices  209 us (34%)
  matrix products  88.6 us (15%)
  local copies, waits for them, and re-layouts  25.7 us (4%)
  other arithmetic  18.5 us (3%)
  between operations  16.8 us (3%)
  blocking collectives  13 us (2%)
    ppermute x36, waiting for transfers between devices, line_scatter(): lax.ppermute(down_sum.astype(jnp.bfloat16), 'gx', [(i, i - 1) for i in ra...  120 us
    ppermute x30, waiting for transfers between devices, line_gather(): from_right.append(lax.ppermute(from_right[-1], 'gx', down_pairs))  92 us
    ppermute x36, starting transfers between devices, line_scatter(): lax.ppermute(up_sum.astype(jnp.bfloat16), 'gx', [(i, i + 1) for i in rang...  80 us
    ppermute x30, starting transfers between devices, line_gather(): from_left.append(lax.ppermute(from_left[-1], 'gx', up_pairs))  58 us
    ppermute x30, starting transfers between devices, line_gather(): from_right.append(lax.ppermute(from_right[-1], 'gx', down_pairs))  38.9 us
    dot_general x48, matrix products, dot_rows(): lax.dot_general(left, right, (((1,), (1,)), ((), ())), preferred_element_...  36.7 us
    dot_general x4, matrix products, body(): upper = jnp.dot(second_normed, up_full, preferred_element_type=jnp.float32)  32.3 us
    ppermute x36, starting transfers between devices, line_scatter(): lax.ppermute(down_sum.astype(jnp.bfloat16), 'gx', [(i, i - 1) for i in ra...  31.7 us
  transfers between devices with their start and end apart: 137, of which 36 were waited for; matrix products, arithmetic and copies ran while one was open for 21% of the time, Pallas kernels for 0%

profile of v1, /device:TPU:0, one launch (start us, length us, event | category | flops | bytes accessed | tf_op | source)
XLA Modules:
  0.0 599.1 jit_solution(10473154650369008929)
XLA Ops:
  10.9 5.0 collective-permute-start
  17.2 7.7 %collective-permute-done = bf16[512,416]{0,1:T(8,128)(2,1)S(1)} collective-permute-done((bf16[512,416]{0,1:T(8,128)(2,1)S(1)}, bf16[512,416]{0,1:T(8,128)(2,1)S(1)}, u32[]{:S(2)}, u32[]{:S(2)}) %collective-permute-start) | collective-permute-done | bytes 426016 | tf_op jit(solution)/shard_map/ppermute | solution.py:45
  31.1 10.5 %collective-permute-done.4 = bf16[512,416]{0,1:T(8,128)(2,1)S(1)} collective-permute-done((bf16[512,416]{0,1:T(8,128)(2,1)S(1)}, bf16[512,416]{0,1:T(8,128)(2,1)S(1)}, u32[]{:S(2)}, u32[]{:S(2)}) %collective-permute-start.4) | collective-permute-done | bytes 426016 | tf_op jit(solution)/shard_map/ppermute | solution.py:46
  43.7 9.6 %collective-permute-done.5 = bf16[512,416]{0,1:T(8,128)(2,1)} collective-permute-done((bf16[512,416]{0,1:T(8,128)(2,1)S(1)}, bf16[512,416]{0,1:T(8,128)(2,1)}, u32[]{:S(2)}, u32[]{:S(2)}) %collective-permute-start.5) | collective-permute-done | bytes 426016 | tf_op jit(solution)/shard_map/ppermute | solution.py:46
  56.8 4.6 collective-permute-start.6
  61.5 4.9 collective-permute-done.9
  71.0 5.7 collective-permute-done.10
  79.4 7.5 %collective-permute-done.11 = bf16[512,416]{0,1:T(8,128)(2,1)S(1)} collective-permute-done((bf16[512,416]{0,1:T(8,128)(2,1)}, bf16[512,416]{0,1:T(8,128)(2,1)S(1)}, u32[]{:S(2)}, u32[]{:S(2)}) %collective-permute-start.11) | collective-permute-done | bytes 426016 | tf_op jit(solution)/shard_map/ppermute | solution.py:46
  89.8 11.3 %copy.49 = bf16[3,1664,416]{1,2,0:T(8,128)(2,1)} copy(bf16[3,1664,416]{2,0,1:T(4,128)(2,1)} %all-gather.6.cloned.1.call-done) | data formatting | bytes 8306688 | tf_op jit(solution)/shard_map/all_gather | solution.py:146
  101.2 4.9 fusion.120
  178.4 33.6 %collective-permute-done.77 = bf16[256,416]{0,1:T(8,128)(2,1)S(1)} collective-permute-done((bf16[256,416]{0,1:T(8,128)(2,1)S(1)}, bf16[256,416]{0,1:T(8,128)(2,1)S(1)}, u32[]{:S(2)}, u32[]{:S(2)}) %collective-permute-start.77) | collective-permute-done | bytes 213024 | tf_op jit(solution)/shard_map/ppermute | solution.py:77
  244.3 4.6 collective-permute-start.78
  250.3 4.6 collective-permute-start.48
  256.1 4.6 collective-permute-start.18
  294.3 9.4 %fusion.35 = bf16[256,2048]{1,0:T(8,128)(2,1)S(1)} fusion(bf16[1664,2048]{1,0:T(8,128)(2,1)} %all-gather.10.cloned.1.call-done, f32[256]{0:T(256)S(1)} %add_rsqrt_fusion.3, f32[256]{0:T(256)S(1)} %broadcast_multiply_fusion.2, f32[1664]{0:T(1024)S(1)} %copy-done.43, f32[1664]{0:T(1024)S(1)} %copy-done.44, bf16[256,416]{0,1:T(8,128)(2,1)S(1)} %get-tuple-element.51, ...), kind=kOutput, calls=%fused_computation.59 | convolution fusion | flops 1784446976 | bytes 8731648 | tf_op jit(solution)/shard_map/dot_general | solution.py:187
  308.2 10.0 %fusion.32 = bf16[256,2048]{1,0:T(8,128)(2,1)S(1)} fusion(bf16[1664,2048]{1,0:T(8,128)(2,1)} %all-gather.10.cloned.1.call-done, f32[256]{0:T(256)S(1)} %add_rsqrt_fusion.5, f32[256]{0:T(256)S(1)} %broadcast_multiply_fusion.3, f32[1664]{0:T(1024)S(1)} %copy-done.43, f32[1664]{0:T(1024)S(1)} %copy-done.44, bf16[256,416]{0,1:T(8,128)(2,1)S(1)} %copy-done.14, ...), kind=kOutput, calls=%fused_computation.56 | convolution fusion | flops 1784446976 | bytes 8731648 | tf_op jit(solution)/shard_map/dot_general | solution.py:187
  320.5 6.5 %fusion.29 = bf16[256,2048]{1,0:T(8,128)(2,1)S(1)} fusion(bf16[1664,2048]{1,0:T(8,128)(2,1)S(1)} %bitcast.226, f32[256]{0:T(256)S(1)} %add_rsqrt_fusion.7, f32[256]{0:T(256)S(1)} %broadcast_multiply_fusion.4, f32[1664]{0:T(1024)S(1)} %copy-done.43, f32[1664]{0:T(1024)S(1)} %copy-done.44, bf16[256,416]{0,1:T(8,128)(2,1)S(1)} %copy-done.22, ...), kind=kOutput, calls=%fused_computation.53 | convolution fusion | flops 1784446976 | bytes 8731648 | tf_op jit(solution)/shard_map/dot_general | solution.py:187
  329.5 6.5 %fusion.26 = bf16[256,2048]{1,0:T(8,128)(2,1)S(1)} fusion(bf16[1664,2048]{1,0:T(8,128)(2,1)S(1)} %bitcast.226, f32[1664]{0:T(1024)S(1)} %copy-done.43, f32[1664]{0:T(1024)S(1)} %copy-done.44, f32[256]{0:T(256)S(1)} %add_rsqrt_fusion.9, f32[256]{0:T(256)S(1)} %broadcast_multiply_fusion.5, bf16[256,416]{0,1:T(8,128)(2,1)S(1)} %copy-done.30, ...), kind=kOutput, calls=%fused_computation.50 | convolution fusion | flops 1784446976 | bytes 8731648 | tf_op jit(solution)/shard_map/dot_general | solution.py:187
  375.7 44.3 %collective-permute-done.119 = bf16[256,416]{0,1:T(8,128)(2,1)S(1)} collective-permute-done((bf16[256,416]{0,1:T(8,128)(2,1)S(1)}, bf16[256,416]{0,1:T(8,128)(2,1)S(1)}, u32[]{:S(2)}, u32[]{:S(2)}) %collective-permute-start.119) | collective-permute-done | bytes 213024 | tf_op jit(solution)/shard_map/ppermute | solution.py:77
  422.9 5.2 collective-permute-start.120
  443.0 6.6 %collective-permute-done.124 = f32[2,256]{1,0:T(2,128)S(1)} collective-permute-done((f32[2,256]{1,0:T(2,128)S(1)}, f32[2,256]{1,0:T(2,128)S(1)}, u32[]{:S(2)}, u32[]{:S(2)}) %collective-permute-start.124) | collective-permute-done | bytes 2080 | tf_op jit(solution)/shard_map/ppermute | solution.py:46
  531.7 5.2 collective-permute-start.128
  542.4 27.4 %collective-permute-done.41 = bf16[64,416]{1,0:T(8,128)(2,1)S(1)} collective-permute-done((bf16[64,416]{1,0:T(8,128)(2,1)S(1)}, bf16[64,416]{1,0:T(8,128)(2,1)S(1)}, u32[]{:S(2)}, u32[]{:S(2)}) %collective-permute-start.41) | collective-permute-done | bytes 53280 | tf_op jit(solution)/shard_map/ppermute | solution.py:77
  578.5 13.0 %all_to_all.5 = bf16[8,64,416]{2,1,0:T(8,128)(2,1)S(1)} all-to-all(bf16[8,64,416]{2,1,0:T(8,128)(2,1)S(1)} %bitcast.174), channel_id=1, replica_groups=mesh['gx'=4,'gy'=8] {'gy'}, dimensions={0} | all-to-all | bytes 851968 | tf_op jit(solution)/shard_map/all_to_all | solution.py:220
  (550 shorter events, 329.2 us)
Async XLA Ops:
  6.5 83.3 %all-gather.6.cloned.1.call-start = ((), (), s32[]{:S(2)}) async-start(), calls=%async_computation.1 | async-start | bytes 7667712 | tf_op jit(solution)/shard_map/all_gather | solution.py:146
  9.2 107.2 %all-gather.8.cloned.1.call-start = ((), (), s32[]{:S(2)}) async-start(), calls=%async_computation.2 | async-start | bytes 1916928 | tf_op jit(solution)/shard_map/all_gather | solution.py:147
  10.1 284.2 %all-gather.10.cloned.1.call-start = ((), (), s32[]{:S(2)}) async-start(), calls=%async_computation.3 | async-start | bytes 7667712 | tf_op jit(solution)/shard_map/all_gather | solution.py:148
  10.8 292.9 %all-gather.12.cloned.1.call-start = ((), (), s32[]{:S(2)}) async-start(), calls=%async_computation.4 | async-start | bytes 7667712 | tf_op jit(solution)/shard_map/all_gather | solution.py:149
  61.4 426.4 %all-gather.14.cloned.1.call-start = ((), (), s32[]{:S(2)}) async-start(), calls=%async_computation.5 | async-start | bytes 6230016 | tf_op jit(solution)/shard_map/all_gather | solution.py:150
  148.9 25.2 %collective-permute-start.74 = (bf16[256,416]{0,1:T(8,128)(2,1)S(1)}, bf16[256,416]{0,1:T(8,128)(2,1)S(1)}, u32[]{:S(2)}, u32[]{:S(2)}) collective-permute-start(bf16[256,416]{0,1:T(8,128)(2,1)S(1)} %get-tuple-element.62), channel_id=1, source_target_pairs={{0,8},{8,16},{16,24},{1,9},{9,17},{17,25},{2,10},{10,18},{18,26},{... | collective-permute-start | bytes 638984 | tf_op jit(solution)/shard_map/ppermute | solution.py:74
  172.7 39.4 %collective-permute-start.77 = (bf16[256,416]{0,1:T(8,128)(2,1)S(1)}, bf16[256,416]{0,1:T(8,128)(2,1)S(1)}, u32[]{:S(2)}, u32[]{:S(2)}) collective-permute-start(bf16[256,416]{0,1:T(8,128)(2,1)S(1)} %add_convert_fusion.16), channel_id=1, source_target_pairs={{8,0},{16,8},{24,16},{9,1},{17,9},{25,17},{10,2},{18,10},{26,18},{... | collective-permute-start | bytes 638984 | tf_op jit(solution)/shard_map/ppermute | solution.py:77
  174.0 41.2 %collective-permute-start.107 = (bf16[256,416]{0,1:T(8,128)(2,1)S(1)}, bf16[256,416]{0,1:T(8,128)(2,1)S(1)}, u32[]{:S(2)}, u32[]{:S(2)}) collective-permute-start(bf16[256,416]{0,1:T(8,128)(2,1)S(1)} %add_convert_fusion.6), channel_id=1, source_target_pairs={{8,0},{16,8},{24,16},{9,1},{17,9},{25,17},{10,2},{18,10},{26,18},{... | collective-permute-start | bytes 638984 | tf_op jit(solution)/shard_map/ppermute | solution.py:77
  175.4 43.5 %collective-permute-start.47 = (bf16[256,416]{0,1:T(8,128)(2,1)S(1)}, bf16[256,416]{0,1:T(8,128)(2,1)S(1)}, u32[]{:S(2)}, u32[]{:S(2)}) collective-permute-start(bf16[256,416]{0,1:T(8,128)(2,1)S(1)} %add_convert_fusion.26), channel_id=1, source_target_pairs={{8,0},{16,8},{24,16},{9,1},{17,9},{25,17},{10,2},{18,10},{26,18},{... | collective-permute-start | bytes 638984 | tf_op jit(solution)/shard_map/ppermute | solution.py:77
  176.7 44.5 %collective-permute-start.17 = (bf16[256,416]{0,1:T(8,128)(2,1)S(1)}, bf16[256,416]{0,1:T(8,128)(2,1)S(1)}, u32[]{:S(2)}, u32[]{:S(2)}) collective-permute-start(bf16[256,416]{0,1:T(8,128)(2,1)S(1)} %add_convert_fusion.36), channel_id=1, source_target_pairs={{8,0},{16,8},{24,16},{9,1},{17,9},{25,17},{10,2},{18,10},{26,18},{... | collective-permute-start | bytes 638984 | tf_op jit(solution)/shard_map/ppermute | solution.py:77
  306.1 37.3 %collective-permute-start.114 = (bf16[256,416]{0,1:T(8,128)(2,1)S(1)}, bf16[256,416]{0,1:T(8,128)(2,1)S(1)}, u32[]{:S(2)}, u32[]{:S(2)}) collective-permute-start(bf16[256,416]{0,1:T(8,128)(2,1)S(1)} %get-tuple-element.132), channel_id=1, source_target_pairs={{0,8},{1,9},{2,10},{3,11},{4,12},{5,13},{6,14},{7,15}} | collective-permute-start | bytes 638984 | tf_op jit(solution)/shard_map/ppermute | solution.py:74
  318.9 26.5 %collective-permute-start.84 = (bf16[256,416]{0,1:T(8,128)(2,1)S(1)}, bf16[256,416]{0,1:T(8,128)(2,1)S(1)}, u32[]{:S(2)}, u32[]{:S(2)}) collective-permute-start(bf16[256,416]{0,1:T(8,128)(2,1)S(1)} %get-tuple-element.128), channel_id=1, source_target_pairs={{0,8},{1,9},{2,10},{3,11},{4,12},{5,13},{6,14},{7,15}} | collective-permute-start | bytes 638984 | tf_op jit(solution)/shard_map/ppermute | solution.py:74
  358.6 63.0 %collective-permute-start.86 = (bf16[256,416]{0,1:T(8,128)(2,1)S(1)}, bf16[256,416]{0,1:T(8,128)(2,1)S(1)}, u32[]{:S(2)}, u32[]{:S(2)}) collective-permute-start(bf16[256,416]{0,1:T(8,128)(2,1)S(1)} %get-tuple-element.60), channel_id=1, source_target_pairs={{0,8},{8,16},{16,24},{1,9},{9,17},{17,25},{2,10},{10,18},{18,26},{... | collective-permute-start | bytes 638984 | tf_op jit(solution)/shard_map/ppermute | solution.py:74
  363.8 64.4 %collective-permute-start.56 = (bf16[256,416]{0,1:T(8,128)(2,1)S(1)}, bf16[256,416]{0,1:T(8,128)(2,1)S(1)}, u32[]{:S(2)}, u32[]{:S(2)}) collective-permute-start(bf16[256,416]{0,1:T(8,128)(2,1)S(1)} %get-tuple-element.56), channel_id=1, source_target_pairs={{0,8},{8,16},{16,24},{1,9},{9,17},{17,25},{2,10},{10,18},{18,26},{... | collective-permute-start | bytes 638984 | tf_op jit(solution)/shard_map/ppermute | solution.py:74
  366.8 67.5 %collective-permute-start.26 = (bf16[256,416]{0,1:T(8,128)(2,1)S(1)}, bf16[256,416]{0,1:T(8,128)(2,1)S(1)}, u32[]{:S(2)}, u32[]{:S(2)}) collective-permute-start(bf16[256,416]{0,1:T(8,128)(2,1)S(1)} %get-tuple-element.52), channel_id=1, source_target_pairs={{0,8},{8,16},{16,24},{1,9},{9,17},{17,25},{2,10},{10,18},{18,26},{... | collective-permute-start | bytes 638984 | tf_op jit(solution)/shard_map/ppermute | solution.py:74
  373.1 47.0 %collective-permute-start.119 = (bf16[256,416]{0,1:T(8,128)(2,1)S(1)}, bf16[256,416]{0,1:T(8,128)(2,1)S(1)}, u32[]{:S(2)}, u32[]{:S(2)}) collective-permute-start(bf16[256,416]{0,1:T(8,128)(2,1)S(1)} %add_convert_fusion.1), channel_id=1, source_target_pairs={{8,0},{16,8},{24,16},{9,1},{17,9},{25,17},{10,2},{18,10},{26,18},{... | collective-permute-start | bytes 638984 | tf_op jit(solution)/shard_map/ppermute | solution.py:77
  374.4 48.4 %collective-permute-start.89 = (bf16[256,416]{0,1:T(8,128)(2,1)S(1)}, bf16[256,416]{0,1:T(8,128)(2,1)S(1)}, u32[]{:S(2)}, u32[]{:S(2)}) collective-permute-start(bf16[256,416]{0,1:T(8,128)(2,1)S(1)} %add_convert_fusion.11), channel_id=1, source_target_pairs={{8,0},{16,8},{24,16},{9,1},{17,9},{25,17},{10,2},{18,10},{26,18},{... | collective-permute-start | bytes 638984 | tf_op jit(solution)/shard_map/ppermute | solution.py:77
  429.6 27.9 %collective-permute-start.90 = (f32[2,256]{1,0:T(2,128)S(1)}, f32[2,256]{1,0:T(2,128)S(1)}, u32[]{:S(2)}, u32[]{:S(2)}) collective-permute-start(f32[2,256]{1,0:T(2,128)S(1)} %pad_maximum_fusion.10), channel_id=1, source_target_pairs={{0,8},{8,16},{16,24},{1,9},{9,17},{17,25},{2,10},{10,18},{18,26},{... | collective-permute-start | bytes 6152 | tf_op jit(solution)/shard_map/ppermute | solution.py:45
  434.3 24.4 %collective-permute-start.93 = (f32[2,256]{1,0:T(2,128)S(1)}, f32[2,256]{1,0:T(2,128)S(1)}, u32[]{:S(2)}, u32[]{:S(2)}) collective-permute-start(f32[2,256]{1,0:T(2,128)S(1)} %pad_maximum_fusion.10), channel_id=1, source_target_pairs={{8,0},{16,8},{24,16},{9,1},{17,9},{25,17},{10,2},{18,10},{26,18},{... | collective-permute-start | bytes 6152 | tf_op jit(solution)/shard_map/ppermute | solution.py:46
  525.8 45.4 %collective-permute-start.68 = (bf16[64,416]{1,0:T(8,128)(2,1)S(1)}, bf16[64,416]{1,0:T(8,128)(2,1)S(1)}, u32[]{:S(2)}, u32[]{:S(2)}) collective-permute-start(bf16[64,416]{1,0:T(8,128)(2,1)S(1)} %get-tuple-element.70), channel_id=1, source_target_pairs={{0,8},{8,16},{16,24},{1,9},{9,17},{17,25},{2,10},{10,18},{18,26},{... | collective-permute-start | bytes 159752 | tf_op jit(solution)/shard_map/ppermute | solution.py:74
  528.4 44.1 %collective-permute-start.98 = (bf16[64,416]{1,0:T(8,128)(2,1)S(1)}, bf16[64,416]{1,0:T(8,128)(2,1)S(1)}, u32[]{:S(2)}, u32[]{:S(2)}) collective-permute-start(bf16[64,416]{1,0:T(8,128)(2,1)S(1)} %get-tuple-element.72), channel_id=1, source_target_pairs={{0,8},{8,16},{16,24},{1,9},{9,17},{17,25},{2,10},{10,18},{18,26},{... | collective-permute-start | bytes 159752 | tf_op jit(solution)/shard_map/ppermute | solution.py:74
  531.7 44.3 %collective-permute-start.128 = (bf16[64,416]{1,0:T(8,128)(2,1)S(1)}, bf16[64,416]{1,0:T(8,128)(2,1)S(1)}, u32[]{:S(2)}, u32[]{:S(2)}) collective-permute-start(bf16[64,416]{1,0:T(8,128)(2,1)S(1)} %get-tuple-element.74), channel_id=1, source_target_pairs={{0,8},{8,16},{16,24},{1,9},{9,17},{17,25},{2,10},{10,18},{18,26},{... | collective-permute-start | bytes 159752 | tf_op jit(solution)/shard_map/ppermute | solution.py:74
  539.8 30.0 %collective-permute-start.41 = (bf16[64,416]{1,0:T(8,128)(2,1)S(1)}, bf16[64,416]{1,0:T(8,128)(2,1)S(1)}, u32[]{:S(2)}, u32[]{:S(2)}) collective-permute-start(bf16[64,416]{1,0:T(8,128)(2,1)S(1)} %add_convert_fusion.56), channel_id=1, source_target_pairs={{8,0},{16,8},{24,16},{9,1},{17,9},{25,17},{10,2},{18,10},{26,18},{... | collective-permute-start | bytes 159752 | tf_op jit(solution)/shard_map/ppermute | solution.py:77
  541.1 31.3 %collective-permute-start.71 = (bf16[64,416]{1,0:T(8,128)(2,1)S(1)}, bf16[64,416]{1,0:T(8,128)(2,1)S(1)}, u32[]{:S(2)}, u32[]{:S(2)}) collective-permute-start(bf16[64,416]{1,0:T(8,128)(2,1)S(1)} %add_convert_fusion.51), channel_id=1, source_target_pairs={{8,0},{16,8},{24,16},{9,1},{17,9},{25,17},{10,2},{18,10},{26,18},{... | collective-permute-start | bytes 159752 | tf_op jit(solution)/shard_map/ppermute | solution.py:77
  (164 other events, 1500.9 us)
Sparse Core Ops, SparseCore 0:
  9.3 50.4 all-gather.5
  61.7 26.2 all-gather.7
  89.9 47.7 all-gather.9
  139.4 47.7 all-gather.11
  236.3 43.2 all-gather.13

commit v2 on v1

v2 whole, which is shorter than its diff:
```python
import functools

import jax
import jax.numpy as jnp
from jax import lax
from jax.experimental import pallas as pl
from jax.experimental.pallas import tpu as pltpu
from jax.sharding import PartitionSpec as P

HEAD = 104
IMG_W = 16
CHUNKS = 4
MESH = pl.DeviceIdType.MESH


EPSILON = 1e-06


def normalize_rows(values, gain, bias):
    values = values.astype(jnp.float32)
    center = values - jnp.mean(values, axis=-1, keepdims=True)
    spread = jnp.mean(center * center, axis=-1, keepdims=True)
    return center * lax.rsqrt(spread + EPSILON) * gain + bias


def normalize_from_sums(values, sums, features, gain, bias):
    values = values.astype(jnp.float32)
    row_mean = sums[0] / features
    spread = sums[1] / features - row_mean * row_mean
    return (values - row_mean[:, None]) * lax.rsqrt(spread[:, None] + EPSILON) * gain + bias


def own_slice(vector, width):
    return lax.dynamic_slice_in_dim(vector, lax.axis_index("gx") * width, width, 0)


def row_sums(values):
    values = values.astype(jnp.float32)
    return jnp.stack([jnp.sum(values, axis=-1), jnp.sum(values * values, axis=-1)])


def line_kernel(count, chunks, size, scatter, gather, has_base, *refs):
    refs = list(refs)
    terms = [refs.pop(0) for _ in range(count)] if scatter else None
    base = refs.pop(0) if has_base else None
    out = refs.pop(0)
    if scatter:
        inbox, scatter_sends, scatter_recvs = refs[0], refs[1], refs[2]
        refs = refs[3:]
    if gather:
        gather_sends, gather_recvs = refs[0], refs[1]
    me = lax.axis_index("gx")
    has_left, has_right = me > 0, me < count - 1
    barrier = pltpu.get_barrier_semaphore()

    @pl.when(has_left)
    def _():
        pl.semaphore_signal(barrier, inc=1, device_id={"gx": me - 1}, device_id_type=MESH)

    @pl.when(has_right)
    def _():
        pl.semaphore_signal(barrier, inc=1, device_id={"gx": me + 1}, device_id_type=MESH)

    @pl.when(has_left & has_right)
    def _():
        pl.semaphore_wait(barrier, 2)

    @pl.when(jnp.logical_not(has_left & has_right))
    def _():
        pl.semaphore_wait(barrier, 1)

    def target(way):
        return {"gx": me + 1 - 2 * way}

    def rows(c):
        return pl.ds(c * size, size)

    def scatter_copy(way, c, d, src):
        return pltpu.make_async_remote_copy(
            src_ref=src,
            dst_ref=inbox.at[way, c, d],
            send_sem=scatter_sends.at[way, c, d],
            recv_sem=scatter_recvs.at[way, c, d],
            device_id=target(way),
            device_id_type=MESH,
        )

    def gather_copy(way, c, j):
        block = out.at[j, rows(c)]
        return pltpu.make_async_remote_copy(
            src_ref=block,
            dst_ref=block,
            send_sem=gather_sends.at[way, c, j],
            recv_sem=gather_recvs.at[way, c, j],
            device_id=target(way),
            device_id_type=MESH,
        )

    def beyond(way, d):
        return me < d if way == 0 else me > d

    def pass_on(c):
        for k in range(count - 1):
            for way in (0, 1):
                d = count - 1 - k if way == 0 else k
                first = me == 0 if way == 0 else me == count - 1

                @pl.when(beyond(way, d) & first)
                def _():
                    scatter_copy(way, c, d, terms[d].at[rows(c)]).start()

                @pl.when(beyond(way, d) & jnp.logical_not(first))
                def _():
                    scatter_copy(way, c, d, inbox.at[way, c, d]).wait_recv()
                    total = inbox[way, c, d].astype(jnp.float32) + terms[d][rows(c)].astype(
                        jnp.float32
                    )
                    inbox[way, c, d] = total.astype(jnp.bfloat16)
                    scatter_copy(way, c, d, inbox.at[way, c, d]).start()

    def settle(c):
        if scatter:
            for d in range(count):

                @pl.when(me == d)
                def _():
                    total = terms[d][rows(c)].astype(jnp.float32)
                    if has_base:
                        total = total + base[rows(c)].astype(jnp.float32)
                    if d > 0:
                        scatter_copy(0, c, d, inbox.at[0, c, d]).wait_recv()
                        total = total + inbox[0, c, d].astype(jnp.float32)
                    if d < count - 1:
                        scatter_copy(1, c, d, inbox.at[1, c, d]).wait_recv()
                        total = total + inbox[1, c, d].astype(jnp.float32)
                    if gather:
                        out[d, rows(c)] = total.astype(jnp.bfloat16)
                    else:
                        out[rows(c)] = total.astype(jnp.bfloat16)
        else:
            out[me, rows(c)] = base[rows(c)]
        if gather:
            for way in (0, 1):

                @pl.when(has_right if way == 0 else has_left)
                def _():
                    gather_copy(way, c, me).start()

    def forward(c, step):
        for way in (0, 1):
            j = me - step if way == 0 else me + step
            held = j >= 0 if way == 0 else j < count

            @pl.when(held)
            def _():
                gather_copy(way, c, j).wait_recv()

                @pl.when(has_right if way == 0 else has_left)
                def _():
                    gather_copy(way, c, j).start()

    lead = 1 if scatter else 0
    for turn in range(chunks + lead + count - 1):
        if scatter and turn < chunks:
            pass_on(turn)
        if 0 <= turn - lead < chunks:
            settle(turn - lead)
        if gather:
            for step in range(1, count):
                if 0 <= turn - lead - step < chunks:
                    forward(turn - lead - step, step)
    for c in range(chunks):
        for way in (0, 1):
            for d in range(count):
                if scatter:

                    @pl.when(beyond(way, d))
                    def _():
                        scatter_copy(way, c, d, inbox.at[way, c, d]).wait_send()

                if gather:
                    sent = (me >= d) & has_right if way == 0 else (me <= d) & has_left

                    @pl.when(sent)
                    def _():
                        gather_copy(way, c, d).wait_send()


def line_call(terms, base, gather, chunks, collective_id):
    count = lax.axis_size("gx")
    scatter = terms is not None
    some = base if base is not None else terms[0]
    rows, width = some.shape
    while rows % (chunks * 16):
        chunks //= 2
    size = rows // chunks
    scratch = []
    if scatter:
        scratch += [
            pltpu.VMEM((2, chunks, count, size, width), jnp.bfloat16),
            pltpu.SemaphoreType.DMA((2, chunks, count)),
            pltpu.SemaphoreType.DMA((2, chunks, count)),
        ]
    if gather:
        scratch += [
            pltpu.SemaphoreType.DMA((2, chunks, count)),
            pltpu.SemaphoreType.DMA((2, chunks, count)),
        ]
    operands = (list(terms) if scatter else []) + ([base] if base is not None else [])
    shape = (count, rows, width) if gather else (rows, width)
    return pl.pallas_call(
        functools.partial(
            line_kernel, count, chunks, size, scatter, gather, base is not None
        ),
        out_shape=jax.ShapeDtypeStruct(shape, jnp.bfloat16),
        in_specs=[pl.BlockSpec(memory_space=pltpu.VMEM)] * len(operands),
        out_specs=pl.BlockSpec(memory_space=pltpu.VMEM),
        scratch_shapes=scratch,
        compiler_params=pltpu.CompilerParams(
            collective_id=collective_id, has_side_effects=True, vmem_limit_bytes=40 * 2**20
        ),
    )(*operands)


def side_by_side(blocks):
    return jnp.concatenate([blocks[j] for j in range(blocks.shape[0])], axis=1)


def dest_terms(left, weight_rows, width):
    return [
        dot_rows(left, weight_rows[d * width : (d + 1) * width]).astype(jnp.bfloat16)
        for d in range(weight_rows.shape[0] // width)
    ]


def dot_rows(left, right):
    return lax.dot_general(
        left, right, (((1,), (1,)), ((), ())), preferred_element_type=jnp.float32
    )


def attend(queries, query_ids, key_rows, value_rows, segment_ids):
    scores = jnp.einsum(
        "qhe,khe->hqk", queries, key_rows, preferred_element_type=jnp.float32
    ) * HEAD ** (-0.5)
    same_segment = query_ids[None, :, None] == segment_ids[None, None, :]
    scores = jnp.where(same_segment, scores, -1e30)
    highest = jnp.max(scores, axis=-1, keepdims=True)
    raised = jnp.exp(scores - highest)
    total = jnp.sum(raised, axis=-1)
    mixed = jnp.einsum(
        "hqk,khe->qhe",
        raised.astype(jnp.bfloat16),
        value_rows,
        preferred_element_type=jnp.float32,
    )
    mixed = (mixed / total.T[:, :, None]).astype(jnp.bfloat16)
    return mixed.reshape(mixed.shape[0], -1)


def body(
    tokens,
    segment_ids,
    first_gain,
    first_bias,
    query_key_value,
    project_out,
    second_gain,
    second_bias,
    up_weight,
    down_weight,
    final_gain,
    final_bias,
    merge_weight,
    owners,
):
    tok_rows = tokens.shape[0]
    width = tokens.shape[1]
    features = width * lax.axis_size("gx")
    qkv_full = lax.all_gather(query_key_value, "gy", axis=1, tiled=True)
    out_rows = lax.all_gather(project_out.T, "gy", axis=0, tiled=True)
    up_full = lax.all_gather(up_weight, "gy", axis=0, tiled=True)
    down_rows = lax.all_gather(down_weight.T, "gy", axis=0, tiled=True)
    merge_rows = lax.all_gather(
        merge_weight.transpose(2, 0, 1).reshape(merge_weight.shape[2], 4 * width),
        "gy",
        axis=0,
        tiled=True,
    )

    full_rows = side_by_side(line_call(None, tokens, True, 1, 0))
    normed = normalize_rows(full_rows, first_gain, first_bias).astype(jnp.bfloat16)
    qkv = jnp.einsum(
        "td,kdc->ktc", normed, qkv_full, preferred_element_type=jnp.float32
    ).astype(jnp.bfloat16)
    head_count = qkv.shape[2] // HEAD
    queries = qkv[0].reshape(tok_rows, head_count, HEAD)
    key_rows = qkv[1].reshape(tok_rows, head_count, HEAD)
    value_rows = qkv[2].reshape(tok_rows, head_count, HEAD)
    query_block = min(512, tok_rows)
    attended = jnp.concatenate(
        [
            attend(
                queries[at : at + query_block],
                segment_ids[at : at + query_block],
                key_rows,
                value_rows,
                segment_ids,
            )
            for at in range(0, tok_rows, query_block)
        ],
        axis=0,
    )
    resid_blocks = line_call(dest_terms(attended, out_rows, width), tokens, True, CHUNKS, 1)
    first_resid = lax.dynamic_index_in_dim(resid_blocks, lax.axis_index("gx"), 0, False)
    second_normed = normalize_rows(
        side_by_side(resid_blocks), second_gain, second_bias
    ).astype(jnp.bfloat16)
    upper = jnp.dot(second_normed, up_full, preferred_element_type=jnp.float32)
    hidden = jax.nn.gelu(upper, approximate=False).astype(jnp.bfloat16)
    second_resid = line_call(dest_terms(hidden, down_rows, width), first_resid, False, CHUNKS, 2)
    post_sums = lax.psum(row_sums(second_resid), "gx")
    final_normed = normalize_from_sums(
        second_resid,
        post_sums,
        features,
        own_slice(final_gain, width),
        own_slice(final_bias, width),
    ).astype(jnp.bfloat16)
    grouped = (
        final_normed.reshape(tok_rows // (2 * IMG_W), 2, IMG_W // 2, 2, width)
        .transpose(0, 2, 1, 3, 4)
        .reshape(tok_rows // 4, 4 * width)
    )
    projected = line_call(dest_terms(grouped, merge_rows, width), None, False, 2, 3)

    merged_rows = tok_rows // 4
    owner_count = lax.axis_size("gy")
    capacity = max(2, 2 * merged_rows // owner_count)
    owner_col = owners[:, 0]
    order = jnp.arange(merged_rows, dtype=jnp.int32)
    earlier = (owner_col[:, None] == owner_col[None, :]) & (order[None, :] < order[:, None])
    slot_rank = jnp.sum(earlier.astype(jnp.int32), axis=1)
    target = owner_col * capacity + slot_rank
    place = (
        jnp.arange(owner_count * capacity, dtype=jnp.int32)[:, None] == target[None, :]
    ).astype(jnp.bfloat16)
    outgoing = jnp.dot(place, projected, preferred_element_type=jnp.float32).astype(jnp.bfloat16)
    outgoing = outgoing.reshape(owner_count, capacity, width)
    arrived = lax.all_to_all(outgoing, "gy", split_axis=0, concat_axis=0, tiled=True)
    return arrived.reshape(1, owner_count, capacity, width)


def solution(mesh):
    in_specs = (
        P("gy", "gx"),
        P("gy"),
        P(),
        P(),
        P(None, "gy", "gx"),
        P("gx", "gy"),
        P(),
        P(),
        P("gy", "gx"),
        P("gx", "gy"),
        P(),
        P(),
        P(None, "gx", "gy"),
        P("gy", None),
    )
    out_specs = P("gy", None, None, "gx")
    return jax.shard_map(body, mesh=mesh, in_specs=in_specs, out_specs=out_specs, check_vma=False)
```

time: 606 us -> 501 us (0.83)
  Pallas kernels: 0 us -> 313 us
  waiting for transfers between devices: 228 us -> 1.36 us
  starting transfers between devices: 209 us -> 0.16 us
  local copies, waits for them, and re-layouts: 25.7 us -> 47.1 us
  blocking collectives: 13 us -> 22.9 us
    pallas_call x0 -> x4, Pallas kernels: none -> 313 us  [line_call(): pl.pallas_call(functools.partial(line_kernel, count, chunks, size, scatte...]
    ppermute x132 -> x0, waiting for transfers between devices: 227 us -> none  [the longest x36 120 us: line_scatter(): lax.ppermute(down_sum.astype(jnp.bfloat16), 'gx', [(i, i - 1) for i in ra...]
    ppermute x132 -> x0, starting transfers between devices: 209 us -> none  [the longest x36 80 us: line_scatter(): lax.ppermute(up_sum.astype(jnp.bfloat16), 'gx', [(i, i + 1) for i in rang...]
    concatenate x0 -> x2, local copies, waits for them, and re-layouts: none -> 12.9 us  [side_by_side(): return jnp.concatenate([blocks[j] for j in range(blocks.shape[0])], axis=1)]
    all_gather x1 -> x0, local copies, waits for them, and re-layouts: 11.3 us -> none  [body(): qkv_full = lax.all_gather(query_key_value, 'gy', axis=1, tiled=True)]
    convert_element_type x4 -> x12, local copies, waits for them, and re-layouts: 0.55 us -> 10.7 us  [dest_terms(): dot_rows(left, weight_rows[d * width:(d + 1) * width]).astype(jnp.bfloat16)]
    psum x0 -> x1, blocking collectives: none -> 8.91 us  [body(): post_sums = lax.psum(row_sums(second_resid), 'gx')]
    unnamed x105 -> x32, local copies, waits for them, and re-layouts: 7.55 us -> 12.7 us
  transfers between devices with their start and end apart: 137 -> 5, of which waited for: 36 -> 0; matrix products, arithmetic and copies ran while one was open for 21% -> 26% of each run, Pallas kernels for 0% -> 57%
where the time goes in v2:
time: 501 us; the launch traced here: 498 us
  Pallas kernels  313 us (62%)
  matrix products  85.5 us (17%)
  local copies, waits for them, and re-layouts  47.1 us (9%)
  blocking collectives  22.9 us (5%)
  between operations  14.1 us (3%)
  other arithmetic  13.7 us (3%)
    pallas_call x4, Pallas kernels, line_call(): pl.pallas_call(functools.partial(line_kernel, count, chunks, size, scatte...  313 us
    dot_general x12, matrix products, dot_rows(): lax.dot_general(left, right, (((1,), (1,)), ((), ())), preferred_element_...  36.2 us
    dot_general x1, matrix products, body(): upper = jnp.dot(second_normed, up_full, preferred_element_type=jnp.float32)  29.8 us
    all_to_all x1, blocking collectives, body(): lax.all_to_all(outgoing, 'gy', split_axis=0, concat_axis=0, tiled=True)  14 us
    concatenate x2, local copies, waits for them, and re-layouts, side_by_side(): return jnp.concatenate([blocks[j] for j in range(blocks.shape[0])], axis=1)  12.9 us
    unnamed x32, local copies, waits for them, and re-layouts  12.7 us
    convert_element_type x12, local copies, waits for them, and re-layouts, dest_terms(): dot_rows(left, weight_rows[d * width:(d + 1) * width]).astype(jnp.bfloat16)  10.7 us
  transfers between devices with their start and end apart: 5, of which 0 were waited for; matrix products, arithmetic and copies ran while one was open for 26% of the time, Pallas kernels for 57%

profile of v2, /device:TPU:0, one launch (start us, length us, event | category | flops | bytes accessed | tf_op | source)
XLA Modules:
  0.0 497.5 jit_solution(957869089188253242)
XLA Ops:
  6.5 2.6 copy.81
  15.3 74.1 %shard_map.136 = bf16[4,1024,416]{2,1,0:T(8,128)(2,1)S(1)} custom-call(bf16[1024,416]{1,0:T(8,128)(2,1)S(1)} %copy.80.refs_0_.refs_4_), custom_call_target="tpu_custom_call" | custom-call | tf_op jit(solution)/shard_map/pallas_call | solution.py:211
  91.1 7.1 %concatenate.9 = bf16[1024,1664]{1,0:T(8,128)(2,1)} concatenate(bf16[1024,416]{1,0:T(8,128)(2,1)} %get-tuple-element.15, bf16[1024,416]{1,0:T(8,128)(2,1)} %get-tuple-element.14, bf16[1024,416]{1,0:T(8,128)(2,1)S(1)} %get-tuple-element.13, bf16[1024,416]{1,0:T(8,128)(2,1)S(1)} %get-tuple-element.12), dimensions={1} | concatenate | bytes 6815744 | tf_op jit(solution)/shard_map/concatenate | solution.py:226
  98.2 2.7 convert_reduce_fusion.1
  100.9 3.0 fusion.20
  106.4 9.7 %convert_bitcast_fusion = bf16[3,1024,416]{1,2,0:T(8,128)(2,1)S(1)} fusion(bf16[3,1664,416]{2,0,1:T(4,128)(2,1)} %all-gather.6.cloned.1.call-done, bf16[1024,1664]{1,0:T(8,128)(2,1)} %concatenate.9, f32[1664]{0:T(1024)S(1)} %copy-done.8, f32[1664]{0:T(1024)S(1)} %copy-done.9, f32[1024]{0:T(1024)S(1)} %add_rsqrt_fusion.2, f32[1024]{0:T(1024)S(1)} %broadcast_multiply_fusion.1), kind=kOutput, calls=%fused_computation.64 | convolution fusion | flops 4264525824 | bytes 10138624 | tf_op jit(solution)/shard_map/td,kdc->ktc/dot_general | solution.py:293
  120.7 4.7 fusion.24
  125.4 2.5 fusion.114
  127.9 2.5 fusion.108
  133.4 2.7 convolution_convert_fusion.1
  137.5 2.8 convolution_convert_fusion.2
  142.5 2.8 convolution_convert_fusion.3
  150.2 137.2 %shard_map.137 = bf16[4,1024,416]{2,1,0:T(8,128)(2,1)S(1)} custom-call(bf16[1024,416]{1,0:T(8,128)(2,1)S(1)} %copy-done.1, bf16[1024,416]{1,0:T(8,128)(2,1)S(1)} %copy-done, bf16[1024,416]{1,0:T(8,128)(2,1)S(1)} %copy.86.refs_2_, bf16[1024,416]{1,0:T(8,128)(2,1)S(1)} %copy.87.refs_3_, bf16[1024,416]{1,0:T(8,128)(2,1)S(1)} %copy.80.refs_0_.refs_4_), custom_call_target="tpu_custom_call" | custom-call | tf_op jit(solution)/shard_map/pallas_call | solution.py:211
  287.4 2.4 dynamic-slice_bitcast_fusion
  289.8 5.8 %concatenate.11 = bf16[1024,1664]{1,0:T(8,128)(2,1)S(1)} concatenate(bf16[1024,416]{1,0:T(8,128)(2,1)} %get-tuple-element.11, bf16[1024,416]{1,0:T(8,128)(2,1)} %get-tuple-element.10, bf16[1024,416]{1,0:T(8,128)(2,1)} %get-tuple-element.9, bf16[1024,416]{1,0:T(8,128)(2,1)} %get-tuple-element.8), dimensions={1} | concatenate | bytes 6815744 | tf_op jit(solution)/shard_map/concatenate | solution.py:226
  297.2 29.8 %fusion.2 = bf16[1024,2048]{1,0:T(8,128)(2,1)} fusion(bf16[1664,2048]{1,0:T(8,128)(2,1)} %all-gather.10.cloned.1.call-done, bf16[1024,1664]{1,0:T(8,128)(2,1)S(1)} %concatenate.11, f32[1664]{0:T(1024)S(1)} %copy-done.10, f32[1664]{0:T(1024)S(1)} %copy-done.11, f32[1024]{0:T(1024)S(1)} %add_rsqrt_fusion.1, f32[1024]{0:T(1024)S(1)} %broadcast_multiply_fusion), kind=kOutput, calls=%fused_computation.7 | convolution fusion | flops 7125860352 | bytes 14439424 | tf_op jit(solution)/shard_map/dot_general | solution.py:319
  327.1 4.7 fusion.67
  332.3 4.7 fusion.70
  337.5 4.7 fusion.73
  343.5 4.7 fusion.76
  353.2 74.0 %shard_map.138 = bf16[1024,416]{1,0:T(8,128)(2,1)S(1)} custom-call(bf16[1024,416]{1,0:T(8,128)(2,1)S(1)} %copy.89.refs_0_, bf16[1024,416]{1,0:T(8,128)(2,1)S(1)} %copy.90.refs_1_, bf16[1024,416]{1,0:T(8,128)(2,1)S(1)} %copy-done.2, bf16[1024,416]{1,0:T(8,128)(2,1)S(1)} %copy-done.3, bf16[1024,416]{1,0:T(8,128)(2,1)S(1)} %copy-done.4), custom_call_target="tpu_custom_call" | custom-call | tf_op jit(solution)/shard_map/pallas_call | solution.py:211
  427.6 8.9 %psum.7 = f32[2,1024]{1,0:T(2,128)S(1)} all-reduce(f32[2,1024]{1,0:T(2,128)S(1)} %pad_maximum_fusion.1), channel_id=1, replica_groups=mesh['gx'=4,'gy'=8] {'gx'}, use_global_device_ids=true, to_apply=%region_11.12 | all-reduce | flops 2048 | bytes 16384 | tf_op jit(solution)/shard_map/psum | solution.py:322
  447.7 27.4 %shard_map.139 = bf16[256,416]{1,0:T(8,128)(2,1)S(1)} custom-call(bf16[256,416]{1,0:T(8,128)(2,1)S(1)} %copy.95.refs_0_, bf16[256,416]{1,0:T(8,128)(2,1)S(1)} %copy.96.refs_1_, bf16[256,416]{1,0:T(8,128)(2,1)S(1)} %copy.97.refs_2_, bf16[256,416]{1,0:T(8,128)(2,1)S(1)} %copy.98.refs_3_), custom_call_target="tpu_custom_call" | custom-call | tf_op jit(solution)/shard_map/pallas_call | solution.py:211
  475.8 14.0 %all_to_all.5 = bf16[8,64,416]{2,1,0:T(8,128)(2,1)S(1)} all-to-all(bf16[8,64,416]{2,1,0:T(8,128)(2,1)S(1)} %bitcast.77), channel_id=1, replica_groups=mesh['gx'=4,'gy'=8] {'gy'}, dimensions={0} | all-to-all | bytes 851968 | tf_op jit(solution)/shard_map/all_to_all | solution.py:350
  (91 shorter events, 47.9 us)
Async XLA Ops:
  6.5 8.2 %copy-start.5 = (bf16[1024,416]{0,1:T(8,128)(2,1)S(1)}, bf16[1024,416]{0,1:T(8,128)(2,1)}, u32[]{:S(2)}) copy-start(bf16[1024,416]{0,1:T(8,128)(2,1)} %param.14) | copy-start | bytes 2555908
  6.5 99.8 %all-gather.6.cloned.1.call-start = ((), (), s32[]{:S(2)}) async-start(), calls=%async_computation.1 | async-start | bytes 7667712 | tf_op jit(solution)/shard_map/all_gather | solution.py:280
  9.2 121.3 %all-gather.8.cloned.1.call-start = ((), (), s32[]{:S(2)}) async-start(), calls=%async_computation.2 | async-start | bytes 1916928 | tf_op jit(solution)/shard_map/all_gather | solution.py:281
  11.0 286.2 %all-gather.10.cloned.1.call-start = ((), (), s32[]{:S(2)}) async-start(), calls=%async_computation.3 | async-start | bytes 7667712 | tf_op jit(solution)/shard_map/all_gather | solution.py:282
  11.8 315.3 %all-gather.12.cloned.1.call-start = ((), (), s32[]{:S(2)}) async-start(), calls=%async_computation.4 | async-start | bytes 7667712 | tf_op jit(solution)/shard_map/all_gather | solution.py:283
  12.3 427.1 %all-gather.14.cloned.1.call-start = ((), (), s32[]{:S(2)}) async-start(), calls=%async_computation.5 | async-start | bytes 6230016 | tf_op jit(solution)/shard_map/all_gather | solution.py:284
  91.0 12.9 %copy-start.6 = (s32[1024]{0:T(1024)S(1)}, s32[1024]{0:T(1024)}, u32[]{:S(2)}) copy-start(s32[1024]{0:T(1024)} %param.15) | copy-start | bytes 12292
  91.0 14.4 %copy-start.7 = (s32[256,1]{0,1:T(1,128)S(1)}, s32[256,1]{0,1:T(1,128)}, u32[]{:S(2)}) copy-start(s32[256,1]{0,1:T(1,128)} %param.27) | copy-start | bytes 3076
  91.0 15.3 %copy-start.8 = (f32[1664]{0:T(1024)S(1)}, f32[1664]{0:T(1024)}, u32[]{:S(2)}) copy-start(f32[1664]{0:T(1024)} %param.17) | copy-start | bytes 19972
  91.1 15.3 %copy-start.9 = (f32[1664]{0:T(1024)S(1)}, f32[1664]{0:T(1024)}, u32[]{:S(2)}) copy-start(f32[1664]{0:T(1024)} %param.16) | copy-start | bytes 19972
  127.9 5.4 %copy-start.12 = (bf16[512,4,104]{0,2,1:T(8,128)(2,1)}, bf16[512,4,104]{0,2,1:T(8,128)(2,1)S(1)}, u32[]{:S(2)}) copy-start(bf16[512,4,104]{0,2,1:T(8,128)(2,1)S(1)} %fusion.114) | copy-start | bytes 1277956
  130.5 0.8 copy-start.13
  147.6 1.4 copy-start
  149.0 1.2 copy-start.1
  289.8 7.4 %copy-start.10 = (f32[1664]{0:T(1024)S(1)}, f32[1664]{0:T(1024)}, u32[]{:S(2)}) copy-start(f32[1664]{0:T(1024)} %param.21) | copy-start | bytes 19972
  289.8 7.4 %copy-start.11 = (f32[1664]{0:T(1024)S(1)}, f32[1664]{0:T(1024)}, u32[]{:S(2)}) copy-start(f32[1664]{0:T(1024)} %param.20) | copy-start | bytes 19972
  349.5 1.2 copy-start.2
  350.7 1.2 copy-start.3
  351.9 1.2 copy-start.4
Sparse Core Ops, SparseCore 0:
  9.3 50.4 all-gather.5
  61.7 26.2 all-gather.7
  89.9 47.7 all-gather.9
  139.4 47.7 all-gather.11
  188.9 42.3 all-gather.13
